TPU v7x, 1024 devices: a whole 8x8x8 slice. The times are simulated.
1024 devices in a mesh: bulk: 64 (over y, x), pair: 16 (over z, core).
Axes of the slice: x: 8, y: 8, z: 8, core: 2. Of those that a mesh axis runs over, the one named last changes fastest.
Arguments:
- amps: bfloat16 [4096, 131072], P(None, ('bulk', 'pair')), may hold values from -6 to 6
- intermediate: bfloat16 [131072, 2048], P('bulk'), may hold values from -0.09375 to 0.09375
- row_irrep: int32 [4096], replicated, may hold values from 0 to 7, as said below
- kc_irrep: int32 [131072], P(('bulk', 'pair')), may hold values from 0 to 7, as said below
- row_occ: int32 [4096], P(('pair', 'bulk')), may hold values from 0 to 249
- row_vir: int32 [4096], P(('pair', 'bulk')), may hold values from 0 to 1499
- col_occ: int32 [2048], replicated, may hold values from 0 to 249
- col_vir: int32 [2048], replicated, may hold values from 0 to 1499
- occ_energy: float32 [250], replicated, may hold values from -1.5 to -0.5
- virt_energy: float32 [1500], replicated, may hold values from 0.5 to 2.5
Outputs:
- panel_update: bfloat16 [4096, 2048], P(('pair', 'bulk'))
Inputs may be any that keep to these rules, and one draw needn't show every extreme that they name: `row_irrep`: constant over aligned blocks of 64 rows; every label 0 to 7 occurs. `kc_irrep`: constant over aligned blocks of 64 pairs; every label 0 to 7 occurs.
All inputs are finite; a program needn't handle non-finite values.
Results may differ from a plain program's by a relative error of at most 0.0013.
Values may be sent and summed in bfloat16 or wider, within the bound.
A program may use at most 32 MiB of HBM per device.

v0:
```python
import jax
import jax.numpy as jnp
from jax import lax
from jax.sharding import PartitionSpec as P


def local(
    amps,
    intermediate,
    row_irrep,
    kc_irrep,
    row_occ,
    row_vir,
    col_occ,
    col_vir,
    occ_energy,
    virt_energy,
):
    kept_mask = row_irrep[:, None] == kc_irrep[None, :]
    masked = jnp.where(kept_mask, amps, jnp.zeros_like(amps))
    groups = lax.axis_size("pair")
    stacked = masked.reshape(groups, masked.shape[0] // groups, masked.shape[1])
    regrouped = lax.all_to_all(stacked, "pair", split_axis=0, concat_axis=2, tiled=True)[0]
    cycle_sums = jnp.dot(regrouped, intermediate, preferred_element_type=jnp.float32)
    panel_share = lax.psum_scatter(cycle_sums, "bulk", scatter_dimension=0, tiled=True)
    row_gap = jnp.take(virt_energy, row_vir) - jnp.take(occ_energy, row_occ)
    col_gap = jnp.take(virt_energy, col_vir) - jnp.take(occ_energy, col_occ)
    denominator = row_gap[:, None] + col_gap[None, :]
    return (panel_share / denominator).astype(jnp.bfloat16)


def solution(mesh):
    return jax.shard_map(
        local,
        mesh=mesh,
        in_specs=(
            P(None, ("bulk", "pair")),
            P("bulk", None),
            P(),
            P(("bulk", "pair")),
            P(("pair", "bulk")),
            P(("pair", "bulk")),
            P(),
            P(),
            P(),
            P(),
        ),
        out_specs=P(("pair", "bulk"), None),
        check_vma=False,
    )
```

profile of v0, /device:TPU:6, one launch (start us, length us, event | category | flops | bytes accessed | tf_op | source)
XLA Modules:
  0.0 242.4 jit_solution(1641294582250841449)
XLA Ops:
  6.5 0.0 copy-start
  6.5 0.0 all-reduce.3.cloned.1.call-start
  6.5 3.0 %compare_select_fusion = bf16[4096,128]{1,0:T(8,128)(2,1)S(1)} fusion(bf16[4096,128]{1,0:T(8,128)(2,1)} %param.10, s32[128]{0:T(128)} %param.13, s32[4096]{0:T(1024)} %param.12), kind=kLoop, calls=%fused_computation.4 | loop fusion | flops 1048576 | bytes 2114048 | tf_op jit(solution)/shard_map/jit(_where)/select_n | solution.py:20
  9.6 43.8 %all_to_all.15 = bf16[16,256,128]{2,1,0:T(8,128)(2,1)S(1)} all-to-all(bf16[16,256,128]{2,1,0:T(8,128)(2,1)S(1)} %bitcast.9), channel_id=1, replica_groups=mesh['bulk'=64,'pair'=16] {'pair'}, dimensions={0} | all-to-all | bytes 2097152 | tf_op jit(solution)/shard_map/all_to_all | solution.py:23
  53.4 0.5 copy.12
  54.0 7.0 %fusion.4 = f32[256,2048]{1,0:T(8,128)} fusion(bf16[256,2048]{0,1:T(8,128)(2,1)S(1)} %bitcast.8, bf16[2048,2048]{1,0:T(8,128)(2,1)} %param.11), kind=kOutput, calls=%fused_computation.19 | convolution fusion | flops 2147483648 | bytes 11534336 | tf_op jit(solution)/shard_map/dot_general | solution.py:24
  61.0 0.0 copy-start.3
  61.0 0.0 all-reduce.3.cloned.1.call-update
  61.0 0.7 copy-done.3
  61.7 0.0 copy-done
  61.7 0.0 copy-start.2
  61.7 11.8 %gather_fusion.2 = f32[2048]{0:T(1024)S(1)} fusion(f32[1500]{0:T(1024)S(1)} %copy-done, s32[2048]{0:T(1024)S(1)} %fusion.1), kind=kCustom, calls=%fused_computation.2 | custom fusion | bytes 24576 | tf_op jit(solution)/shard_map/jit(_take)/gather | solution.py:27
  73.5 0.0 copy-done.4
  73.5 0.0 copy-start.1
  73.6 0.6 gather_fusion
  74.2 0.0 copy-done.2
  74.2 0.0 copy-done.1
  74.2 0.0 copy-start.5
  74.2 13.1 %gather_fusion.3 = f32[2048]{0:T(1024)S(1)} fusion(f32[250]{0:T(256)S(1)} %copy-done.1, s32[2048]{0:T(1024)S(1)} %fusion.2), kind=kCustom, calls=%fused_computation.3 | custom fusion | bytes 24576 | tf_op jit(solution)/shard_map/jit(_take)/gather | solution.py:27
  87.4 0.0 copy-done.5
  87.4 0.6 gather_fusion.1
  88.1 1.3 dynamic-slice
  90.0 144.0 %all-reduce.3.cloned.1.call-done = f32[256,2048]{1,0:T(8,128)} async-done(((f32[256,2048]{1,0:T(8,128)}), f32[256,2048]{1,0:T(8,128)}) %all-reduce.3.cloned.1.call-update) | async-done | bytes 2097168
  234.0 1.5 fusion
  (9 shorter events, 0.0 us)
Async XLA Ops:
  6.5 55.2 %copy-start = (f32[1500]{0:T(1024)S(1)}, f32[1500]{0:T(1024)}, u32[]{:S(2)}) copy-start(f32[1500]{0:T(1024)} %param.19) | copy-start | bytes 18004
  6.5 227.5 %all-reduce.3.cloned.1.call-start = ((), (), s32[]{:S(2)}) async-start(), calls=%async_computation.1 | async-start | bytes 4194304
  61.0 0.7 copy-start.3
  61.7 11.8 %copy-start.4 = (s32[4]{0:T(128)S(1)}, s32[4]{0:T(128)}, u32[]{:S(2)}) copy-start(s32[4]{0:T(128)} %param.15) | copy-start | bytes 52
  61.7 12.5 %copy-start.2 = (s32[2048]{0:T(1024)S(1)}, s32[2048]{0:T(1024)}, u32[]{:S(2)}) copy-start(s32[2048]{0:T(1024)} %param.16) | copy-start | bytes 24580
  73.5 0.7 copy-start.1
  74.2 13.2 %copy-start.5 = (s32[4]{0:T(128)S(1)}, s32[4]{0:T(128)}, u32[]{:S(2)}) copy-start(s32[4]{0:T(128)} %param.14) | copy-start | bytes 52
Sparse Core Ops, SparseCore 0:
  61.2 172.8 all-reduce.2
where the time goes:
time: 243 us; the launch traced here: 242 us
  waiting for transfers between devices  144 us (59%)
  blocking collectives  43.8 us (18%)
  local copies, waits for them, and re-layouts  28.7 us (12%)
  between operations  14.2 us (6%)
  matrix products  7.04 us (3%)
  other arithmetic  4.62 us (2%)
    unnamed x2, waiting for transfers between devices  144 us
    all_to_all x1, blocking collectives, local(): lax.all_to_all(stacked, 'pair', split_axis=0, concat_axis=2, tiled=True)[0]  43.8 us
    gather x2, local copies, waits for them, and re-layouts, local(): col_gap = jnp.take(virt_energy, col_vir) - jnp.take(occ_energy, col_occ)  24.9 us
    dot_general x1, matrix products, local(): jnp.dot(regrouped, intermediate, preferred_element_type=jnp.float32)  7.04 us
  transfers between devices with their start and end apart: 1, of which 1 were waited for; matrix products, arithmetic and copies ran while one was open for 11% of the time, Pallas kernels for 0%

commit v1 on v0

v1 whole, which is shorter than its diff:
```python
import functools

import jax
import jax.numpy as jnp
from jax import lax
from jax.experimental import pallas as pl
from jax.experimental.pallas import tpu as pltpu
from jax.sharding import PartitionSpec as P

MESH = pl.DeviceIdType.MESH
F32 = jnp.float32
BF16 = jnp.bfloat16

SIDE = 8
PAIRS = 16
ROWS = 4
PLANE = SIDE * SIDE
LANES = 128
IRB = 64


def split_gather(table, labels):
    size = table.shape[1]
    whole = jnp.broadcast_to(table, (16, size))
    high = whole.astype(BF16).astype(F32)
    rest = whole - high
    middle = rest.astype(BF16).astype(F32)
    low = rest - middle
    part = lax.broadcasted_iota(jnp.int32, (16, size), 0)
    parts = jnp.where(part == 0, high, jnp.where(part == 1, middle, jnp.where(part == 2, low, 0.0))).astype(BF16)
    place = lax.broadcasted_iota(jnp.int32, (size, labels.shape[1]), 0)
    chosen = jnp.where(place == labels, 1.0, 0.0).astype(BF16)
    got = jnp.dot(parts, chosen, preferred_element_type=F32)
    return got[0:1, :] + (got[1:2, :] + got[2:3, :])


def kernel(
    amps_hbm,
    weights_hbm,
    row_irrep,
    kc_irrep,
    row_occ,
    row_vir,
    col_occ,
    col_vir,
    occ_scalar,
    virt_scalar,
    occ_vector,
    virt_vector,
    out_ref,
    amps,
    weights,
    outgoing,
    regrouped,
    sums,
    first_in,
    first_out,
    second_in,
    panel,
    virt_table,
    occ_table,
    col_gap,
    amps_sem,
    weights_sem,
    pair_send,
    pair_recv,
    first_send,
    first_recv,
    second_send,
    second_recv,
):
    bulk = lax.axis_index("bulk")
    pair = lax.axis_index("pair")
    at_y, at_x = lax.div(bulk, SIDE), lax.rem(bulk, SIDE)
    columns = weights.shape[1]

    amps_copy = pltpu.make_async_copy(amps_hbm, amps, amps_sem)
    amps_copy.start()
    weights_copy = pltpu.make_async_copy(weights_hbm, weights, weights_sem)
    weights_copy.start()

    def pair_peer(step):
        return lax.rem(pair + step, PAIRS)

    def x_peer(step):
        return at_y * SIDE + lax.rem(at_x + step, SIDE)

    def y_peer(step):
        return lax.rem(at_y + step, SIDE) * SIDE + at_x

    barrier = pltpu.get_barrier_semaphore()

    @pl.loop(1, PAIRS)
    def _(step):
        pl.semaphore_signal(barrier, inc=1, device_id=(bulk, pair_peer(step)), device_id_type=MESH)

    @pl.loop(1, SIDE)
    def _(step):
        pl.semaphore_signal(barrier, inc=1, device_id=(x_peer(step), pair), device_id_type=MESH)
        pl.semaphore_signal(barrier, inc=1, device_id=(y_peer(step), pair), device_id_type=MESH)

    block = ROWS * PLANE
    new_place = lax.broadcasted_iota(jnp.int32, (block, block), 0)
    old_place = lax.broadcasted_iota(jnp.int32, (block, block), 1)
    chunk_of = new_place >> 6
    outer, inner = (new_place >> 3) & 7, new_place & 7
    even = (chunk_of & 1) == 0
    y_of, x_of = jnp.where(even, inner, outer), jnp.where(even, outer, inner)
    reorder = jnp.where(old_place == y_of * (SIDE * ROWS) + x_of * ROWS + chunk_of, 1.0, 0.0).astype(BF16)
    kc = kc_irrep[...]

    amps_copy.wait()
    pl.semaphore_wait(barrier, PAIRS - 1 + 2 * (SIDE - 1))

    def pair_copy(chunk, step):
        peer = pair_peer(step)
        return pltpu.make_async_remote_copy(
            src_ref=outgoing.at[chunk, peer],
            dst_ref=regrouped.at[chunk, :, pl.ds(pl.multiple_of(pair * LANES, LANES), LANES)],
            send_sem=pair_send.at[chunk, step],
            recv_sem=pair_recv.at[chunk, pair],
            device_id=(bulk, peer),
            device_id_type=MESH,
        )

    def pair_arrival(chunk, step):
        source = pair_peer(step)
        return pltpu.make_async_remote_copy(
            src_ref=outgoing.at[chunk, source],
            dst_ref=regrouped.at[chunk, :, pl.ds(pl.multiple_of(source * LANES, LANES), LANES)],
            send_sem=pair_send.at[chunk, step],
            recv_sem=pair_recv.at[chunk, source],
            device_id=(bulk, source),
            device_id_type=MESH,
        )

    def prepare(owner):
        kept = []
        for part in range(block // IRB):
            label = row_irrep[owner * block + part * IRB]
            keep = jnp.where(kc == label, 1.0, 0.0)
            begin = pl.multiple_of(owner * block + part * IRB, IRB)
            kept.append((amps[pl.ds(begin, IRB), :].astype(F32) * keep).astype(BF16))
        moved = jnp.dot(reorder, jnp.concatenate(kept, axis=0), preferred_element_type=F32).astype(BF16)
        for chunk in range(ROWS):
            outgoing[chunk, owner] = moved[chunk * PLANE : (chunk + 1) * PLANE, :]

    @pl.loop(1, PAIRS)
    def _(step):
        prepare(pair_peer(step))
        pair_copy(0, step).start()

    for chunk in range(1, ROWS):

        @pl.loop(1, PAIRS)
        def _(step):
            pair_copy(chunk, step).start()

    prepare(pair)
    for chunk in range(ROWS):
        regrouped[chunk, :, pl.ds(pl.multiple_of(pair * LANES, LANES), LANES)] = outgoing[chunk, pair]

    virt_table[...] = jnp.zeros_like(virt_table)
    occ_table[...] = jnp.zeros_like(occ_table)
    virt_table[:, 0 : virt_vector.shape[1]] = virt_vector[...]
    occ_table[:, 0 : occ_vector.shape[1]] = occ_vector[...]
    width = 256

    @pl.loop(0, columns // width)
    def _(tile):
        where = pl.ds(pl.multiple_of(tile * width, width), width)
        col_gap[:, where] = split_gather(virt_table[...], col_vir[:, where]) - split_gather(occ_table[...], col_occ[:, where])

    weights_copy.wait()

    def first_copy(chunk, step, arrival=False):
        mine = at_x if chunk % 2 == 0 else at_y
        to = lax.rem(mine + step, SIDE)
        source = to if arrival else mine
        return pltpu.make_async_remote_copy(
            src_ref=sums.at[chunk, pl.ds(pl.multiple_of(to * SIDE, SIDE), SIDE), :],
            dst_ref=first_in.at[chunk, source],
            send_sem=first_send.at[chunk, step],
            recv_sem=first_recv.at[chunk, source],
            device_id=(x_peer(step) if chunk % 2 == 0 else y_peer(step), pair),
            device_id_type=MESH,
        )

    def second_copy(chunk, step, arrival=False):
        mine = at_y if chunk % 2 == 0 else at_x
        to = lax.rem(mine + step, SIDE)
        source = to if arrival else mine
        return pltpu.make_async_remote_copy(
            src_ref=first_out.at[chunk, pl.ds(pl.multiple_of(to * 16, 16), 16), :],
            dst_ref=second_in.at[chunk, source],
            send_sem=second_send.at[chunk, step],
            recv_sem=second_recv.at[chunk, source],
            device_id=(y_peer(step) if chunk % 2 == 0 else x_peer(step), pair),
            device_id_type=MESH,
        )

    def multiply(chunk):
        @pl.loop(1, PAIRS)
        def _(step):
            pair_arrival(chunk, step).wait_recv()

        @pl.loop(0, columns // width)
        def _(tile):
            where = pl.ds(pl.multiple_of(tile * width, width), width)
            sums[chunk, :, where] = jnp.dot(regrouped[chunk], weights[:, where], preferred_element_type=F32)

        @pl.loop(1, SIDE)
        def _(step):
            first_copy(chunk, step).start()

    def add_first(chunk):
        @pl.loop(1, SIDE)
        def _(step):
            first_copy(chunk, step, arrival=True).wait_recv()

        mine = at_x if chunk % 2 == 0 else at_y
        first_in[chunk, mine] = sums[chunk, pl.ds(pl.multiple_of(mine * SIDE, SIDE), SIDE), :]
        for tile in range(columns // LANES):
            lanes = slice(tile * LANES, (tile + 1) * LANES)
            total = first_in[chunk, 0, :, lanes]
            for source in range(1, SIDE):
                total = total + first_in[chunk, source, :, lanes]
            first_out[chunk, pl.ds(tile, SIDE, stride=16), :] = total

        @pl.loop(1, SIDE)
        def _(step):
            second_copy(chunk, step).start()

    def add_second(chunk):
        @pl.loop(1, SIDE)
        def _(step):
            second_copy(chunk, step, arrival=True).wait_recv()

        mine = at_y if chunk % 2 == 0 else at_x
        second_in[chunk, mine] = first_out[chunk, pl.ds(pl.multiple_of(mine * 16, 16), 16), :]
        total = second_in[chunk, 0]
        for source in range(1, SIDE):
            total = total + second_in[chunk, source]
        panel[chunk * 16 : (chunk + 1) * 16, :] = total

    for turn in range(ROWS + 2):
        if turn < ROWS:
            multiply(turn)
        if 0 <= turn - 1 < ROWS:
            add_first(turn - 1)
        if 0 <= turn - 2 < ROWS:
            add_second(turn - 2)

    row = lax.broadcasted_iota(jnp.int32, (ROWS, columns), 0)
    row_gap = jnp.zeros((ROWS, columns), F32)
    for r in range(ROWS):
        row_gap = jnp.where(row == r, virt_scalar[row_vir[r]] - occ_scalar[row_occ[r]], row_gap)
    cycle = jnp.concatenate([panel[pl.ds(tile, ROWS, stride=16), :] for tile in range(columns // LANES)], axis=1)
    out_ref[...] = cycle / (row_gap + col_gap[...])

    for chunk in range(ROWS):

        @pl.loop(1, PAIRS)
        def _(step):
            pair_copy(chunk, step).wait_send()

        @pl.loop(1, SIDE)
        def _(step):
            first_copy(chunk, step).wait_send()
            second_copy(chunk, step).wait_send()


def local(
    amps,
    intermediate,
    row_irrep,
    kc_irrep,
    row_occ,
    row_vir,
    col_occ,
    col_vir,
    occ_energy,
    virt_energy,
):
    depth, columns = intermediate.shape
    vmem = pl.BlockSpec(memory_space=pltpu.VMEM)
    smem = pl.BlockSpec(memory_space=pltpu.SMEM)
    anywhere = pl.BlockSpec(memory_space=pl.ANY)
    dma = pltpu.SemaphoreType.DMA
    panel_update = pl.pallas_call(
        kernel,
        out_shape=jax.ShapeDtypeStruct((ROWS, columns), F32),
        in_specs=[anywhere, anywhere, smem, vmem, smem, smem, vmem, vmem, smem, smem, vmem, vmem],
        out_specs=vmem,
        scratch_shapes=[
            pltpu.VMEM(amps.shape, BF16),
            pltpu.VMEM((depth, columns), BF16),
            pltpu.VMEM((ROWS, PAIRS, PLANE, LANES), BF16),
            pltpu.VMEM((ROWS, PLANE, depth), BF16),
            pltpu.VMEM((ROWS, PLANE, columns), F32),
            pltpu.VMEM((ROWS, SIDE, SIDE, columns), F32),
            pltpu.VMEM((ROWS, SIDE * 16, LANES), F32),
            pltpu.VMEM((ROWS, SIDE, 16, LANES), F32),
            pltpu.VMEM((ROWS * 16, LANES), F32),
            pltpu.VMEM((1, 1536), F32),
            pltpu.VMEM((1, 256), F32),
            pltpu.VMEM((1, columns), F32),
            dma,
            dma,
            dma((ROWS, PAIRS)),
            dma((ROWS, PAIRS)),
            dma((ROWS, SIDE)),
            dma((ROWS, SIDE)),
            dma((ROWS, SIDE)),
            dma((ROWS, SIDE)),
        ],
        compiler_params=pltpu.CompilerParams(
            collective_id=0, has_side_effects=True, vmem_limit_bytes=40 * 1024 * 1024
        ),
        cost_estimate=pl.CostEstimate(flops=2 * amps.shape[0] * amps.shape[1] * columns, bytes_accessed=9 << 20, transcendentals=0),
    )(
        amps,
        intermediate,
        row_irrep,
        kc_irrep[None, :],
        row_occ,
        row_vir,
        col_occ[None, :],
        col_vir[None, :],
        occ_energy,
        virt_energy,
        occ_energy[None, :],
        virt_energy[None, :],
    )
    return panel_update.astype(BF16)


def solution(mesh):
    return jax.shard_map(
        local,
        mesh=mesh,
        in_specs=(
            P(None, ("bulk", "pair")),
            P("bulk", None),
            P(),
            P(("bulk", "pair")),
            P(("pair", "bulk")),
            P(("pair", "bulk")),
            P(),
            P(),
            P(),
            P(),
        ),
        out_specs=P(("pair", "bulk"), None),
        check_vma=False,
    )
```

time: 243 us -> 94.8 us (0.39)
  the two profiles are of different devices: /device:TPU:6 before, /device:TPU:32 now
where the time goes in v1:
time: 94.8 us; the launch traced here: 94.3 us
  Pallas kernels  82.9 us (87%)
  local copies, waits for them, and re-layouts  10.8 us (11%)
    pallas_call x1, Pallas kernels, local(): pl.pallas_call(kernel, out_shape=jax.ShapeDtypeStruct((ROWS, columns), F3...  82.9 us
    unnamed x20, local copies, waits for them, and re-layouts  10.1 us

profile of v1, /device:TPU:32, one launch (start us, length us, event | category | flops | bytes accessed | tf_op | source)
XLA Modules:
  0.0 94.3 jit_solution(6653543177275856344)
XLA Ops:
  0.0 0.7 broadcast_in_dim.19.virt_vector
  0.7 0.0 copy-start
  0.7 3.4 %copy-done = bf16[2048,2048]{1,0:T(8,128)(2,1)S(1)} copy-done((bf16[2048,2048]{1,0:T(8,128)(2,1)S(1)}, bf16[2048,2048]{1,0:T(8,128)(2,1)}, u32[]{:S(2)}) %copy-start) | copy-done | bytes 8388632
  4.1 0.0 copy-start.1
  4.1 1.2 %copy-done.1 = bf16[4096,128]{1,0:T(8,128)(2,1)S(1)} copy-done((bf16[4096,128]{1,0:T(8,128)(2,1)S(1)}, bf16[4096,128]{1,0:T(8,128)(2,1)}, u32[]{:S(2)}) %copy-start.1) | copy-done | bytes 1048600
  5.3 0.0 copy-start.2
  5.3 0.7 copy-done.2
  6.0 0.0 copy-start.3
  6.0 0.7 copy-done.3
  6.7 0.0 copy-start.4
  6.7 0.7 copy-done.4
  7.4 0.0 copy-start.5
  7.4 0.7 copy-done.5
  8.1 0.0 copy-start.6
  8.1 0.7 copy-done.6
  8.8 0.0 copy-start.7
  8.8 0.7 copy-done.7
  9.5 0.0 copy-start.8
  9.5 0.7 copy-done.8
  10.1 0.0 copy-start.9
  10.1 0.7 copy-done.9
  10.8 82.9 %shard_map.100 = f32[4,2048]{1,0:T(4,128)S(1)} custom-call(bf16[4096,128]{1,0:T(8,128)(2,1)S(1)} %copy-done.1, bf16[2048,2048]{1,0:T(8,128)(2,1)S(1)} %copy-done, s32[4096]{0:T(1024)S(1)} %copy-done.3, s32[1,128]{1,0:T(1,128)S(1)} %bitcast.7, s32[4]{0:T(128)S(1)} %copy-done.8, s32[4]{0:T(128)S(1)} %copy-done.9, s32[1,2048]{1,0:T(1,128)S(1)} %bitcast.4, ...), custom_call_target="tpu_custom_call" | custom-call | flops 2147483648 | bytes 9437184 | tf_op jit(solution)/shard_map/pallas_call | solution.py:290
  93.7 0.6 convert_element_type.3
Async XLA Ops:
  0.7 3.4 %copy-start = (bf16[2048,2048]{1,0:T(8,128)(2,1)S(1)}, bf16[2048,2048]{1,0:T(8,128)(2,1)}, u32[]{:S(2)}) copy-start(bf16[2048,2048]{1,0:T(8,128)(2,1)} %weights_hbm.1) | copy-start | bytes 25165828
  4.1 1.2 %copy-start.1 = (bf16[4096,128]{1,0:T(8,128)(2,1)S(1)}, bf16[4096,128]{1,0:T(8,128)(2,1)}, u32[]{:S(2)}) copy-start(bf16[4096,128]{1,0:T(8,128)(2,1)} %amps_hbm.1) | copy-start | bytes 3145732
  5.3 0.7 copy-start.2
  6.0 0.7 copy-start.3
  6.7 0.7 copy-start.4
  7.4 0.7 copy-start.5
  8.1 0.7 copy-start.6
  8.8 0.7 copy-start.7
  9.5 0.7 copy-start.8
  10.1 0.7 copy-start.9

commit v2 on v1

v2 whole, which is shorter than its diff:
```python
import functools

import jax
import jax.numpy as jnp
from jax import lax
from jax.experimental import pallas as pl
from jax.experimental.pallas import tpu as pltpu
from jax.sharding import PartitionSpec as P

MESH = pl.DeviceIdType.MESH
F32 = jnp.float32
BF16 = jnp.bfloat16

SIDE = 8
PAIRS = 16
ROWS = 4
PLANE = SIDE * SIDE
LANES = 128
IRB = 64
CODES = 32767.0


def split_gather(table, labels):
    size = table.shape[1]
    whole = jnp.broadcast_to(table, (16, size))
    high = whole.astype(BF16).astype(F32)
    rest = whole - high
    middle = rest.astype(BF16).astype(F32)
    low = rest - middle
    part = lax.broadcasted_iota(jnp.int32, (16, size), 0)
    parts = jnp.where(part == 0, high, jnp.where(part == 1, middle, jnp.where(part == 2, low, 0.0))).astype(BF16)
    place = lax.broadcasted_iota(jnp.int32, (size, labels.shape[1]), 0)
    chosen = jnp.where(place == labels, 1.0, 0.0).astype(BF16)
    got = jnp.dot(parts, chosen, preferred_element_type=F32)
    return got[0:1, :] + (got[1:2, :] + got[2:3, :])


def kernel(
    amps_hbm,
    weights_hbm,
    row_irrep_hbm,
    kc_irrep_hbm,
    row_occ_hbm,
    row_vir_hbm,
    col_occ_hbm,
    col_vir_hbm,
    occ_hbm,
    virt_hbm,
    out_ref,
    row_irrep,
    kc_irrep,
    row_occ,
    row_vir,
    col_occ,
    col_vir,
    occ_scalar,
    virt_scalar,
    occ_vector,
    virt_vector,
    amps,
    weights,
    outgoing,
    regrouped,
    sums_x,
    sums_y,
    coded_out,
    coded_in,
    scale_out,
    scale_in,
    first_out,
    second_in,
    panel,
    virt_table,
    occ_table,
    col_gap,
    small_sem,
    amps_sem,
    weights_sem,
    pair_send,
    pair_recv,
    coded_send,
    coded_recv,
    scale_send,
    scale_recv,
    second_send,
    second_recv,
):
    bulk = lax.axis_index("bulk")
    pair = lax.axis_index("pair")
    at_y, at_x = lax.div(bulk, SIDE), lax.rem(bulk, SIDE)
    columns = weights.shape[1]

    amps_copy = pltpu.make_async_copy(amps_hbm, amps, amps_sem)
    amps_copy.start()
    small = [
        (row_irrep_hbm, row_irrep),
        (kc_irrep_hbm, kc_irrep),
        (row_occ_hbm, row_occ),
        (row_vir_hbm, row_vir),
        (col_occ_hbm, col_occ),
        (col_vir_hbm, col_vir),
        (occ_hbm, occ_scalar),
        (virt_hbm, virt_scalar),
        (occ_hbm, occ_vector),
        (virt_hbm, virt_vector),
    ]
    small_copies = [pltpu.make_async_copy(a, b, small_sem.at[i]) for i, (a, b) in enumerate(small)]
    for copy in small_copies:
        copy.start()
    weights_copy = pltpu.make_async_copy(weights_hbm, weights, weights_sem)
    weights_copy.start()

    def pair_peer(step):
        return lax.rem(pair + step, PAIRS)

    def x_peer(step):
        return at_y * SIDE + lax.rem(at_x + step, SIDE)

    def y_peer(step):
        return lax.rem(at_y + step, SIDE) * SIDE + at_x

    barrier = pltpu.get_barrier_semaphore()

    @pl.loop(1, PAIRS)
    def _(step):
        pl.semaphore_signal(barrier, inc=1, device_id=(bulk, pair_peer(step)), device_id_type=MESH)

    @pl.loop(1, SIDE)
    def _(step):
        pl.semaphore_signal(barrier, inc=1, device_id=(x_peer(step), pair), device_id_type=MESH)
        pl.semaphore_signal(barrier, inc=1, device_id=(y_peer(step), pair), device_id_type=MESH)

    block = ROWS * PLANE
    new_place = lax.broadcasted_iota(jnp.int32, (block, block), 0)
    old_place = lax.broadcasted_iota(jnp.int32, (block, block), 1)
    chunk_of, x_of, y_of = new_place >> 6, (new_place >> 3) & 7, new_place & 7
    reorder = jnp.where(old_place == y_of * (SIDE * ROWS) + x_of * ROWS + chunk_of, 1.0, 0.0).astype(BF16)
    for copy in small_copies[:2]:
        copy.wait()
    kc = kc_irrep[...]

    amps_copy.wait()

    def prepare(owner):
        kept = []
        for part in range(block // IRB):
            label = row_irrep[owner * block + part * IRB]
            keep = jnp.where(kc == label, 1.0, 0.0)
            begin = pl.multiple_of(owner * block + part * IRB, IRB)
            kept.append((amps[pl.ds(begin, IRB), :].astype(F32) * keep).astype(BF16))
        moved = jnp.dot(reorder, jnp.concatenate(kept, axis=0), preferred_element_type=F32).astype(BF16)
        for chunk in range(ROWS):
            outgoing[chunk, owner] = moved[chunk * PLANE : (chunk + 1) * PLANE, :]

    @pl.loop(0, PAIRS)
    def _(owner):
        prepare(owner)

    pl.semaphore_wait(barrier, PAIRS - 1 + 2 * (SIDE - 1))

    mine_columns = pl.ds(pl.multiple_of(pair * LANES, LANES), LANES)

    for chunk in range(ROWS):

        @pl.loop(1, PAIRS)
        def _(step):
            peer = pair_peer(step)
            pltpu.make_async_remote_copy(
                src_ref=outgoing.at[chunk, peer],
                dst_ref=regrouped.at[chunk, :, mine_columns],
                send_sem=pair_send.at[chunk],
                recv_sem=pair_recv.at[chunk],
                device_id=(bulk, peer),
                device_id_type=MESH,
            ).start()

    def all_of(ref, count, send_sem, recv_sem):
        part = ref.at[pl.ds(0, count)]
        return pltpu.make_async_remote_copy(
            src_ref=part, dst_ref=part, send_sem=send_sem, recv_sem=recv_sem, device_id=(bulk, pair_peer(1)), device_id_type=MESH
        )

    def all_pairs(chunk):
        return all_of(outgoing.at[chunk], PAIRS - 1, pair_send.at[chunk], pair_recv.at[chunk])

    for chunk in range(ROWS):
        regrouped[chunk, :, mine_columns] = outgoing[chunk, pair]

    for copy in small_copies[2:]:
        copy.wait()
    virt_table[...] = jnp.zeros_like(virt_table)
    occ_table[...] = jnp.zeros_like(occ_table)
    virt_table[:, 0 : virt_vector.shape[0]] = virt_vector[...].reshape(1, virt_vector.shape[0])
    occ_table[:, 0 : occ_vector.shape[0]] = occ_vector[...].reshape(1, occ_vector.shape[0])
    width = 256

    @pl.loop(0, columns // width)
    def _(tile):
        where = pl.ds(pl.multiple_of(tile * width, width), width)
        col_gap[:, where] = split_gather(virt_table[...], col_vir[:, where]) - split_gather(occ_table[...], col_occ[:, where])

    weights_copy.wait()

    half_width = columns // 2
    tiles = half_width // LANES

    def along(half, step):
        return x_peer(step) if half == 0 else y_peer(step)

    def place(half):
        return at_x if half == 0 else at_y

    def multiply(chunk, half):
        @pl.loop(0, half_width // width)
        def _(tile):
            where = pl.ds(pl.multiple_of(half * half_width + tile * width, width), width)
            product = jnp.dot(regrouped[chunk], weights[:, where], preferred_element_type=F32)
            if half == 0:
                sums_x[chunk, :, pl.ds(pl.multiple_of(tile * width, width), width)] = product
            else:
                for part in range(width // LANES):
                    sums_y[chunk, tile * (width // LANES) + part] = product[:, part * LANES : (part + 1) * LANES]

    def pieces(chunk, half, to):
        if half == 0:
            rows = pl.ds(pl.multiple_of(to * SIDE, SIDE), SIDE)
            return [sums_x[chunk, rows, tile * LANES : (tile + 1) * LANES] for tile in range(tiles)]
        return [sums_y[chunk, tile, pl.ds(to, SIDE, stride=SIDE), :] for tile in range(tiles)]

    def send_first(chunk, half):
        whole = sums_x[chunk] if half == 0 else sums_y[chunk].reshape(tiles * PLANE, LANES)
        top = jnp.maximum(jnp.max(jnp.abs(whole), axis=(0, 1), keepdims=True), 1e-33)
        scale_out[chunk, half] = jnp.broadcast_to(top * (1.0 / CODES), (1, LANES))
        factor = jnp.broadcast_to(CODES / top, (2 * SIDE, LANES))

        @pl.loop(1, SIDE)
        def _(step):
            to = lax.rem(place(half) + step, SIDE)
            given = pieces(chunk, half, to)
            for tile in range(tiles // 2):
                pair_of = jnp.concatenate([given[tile], given[tile + tiles // 2]], axis=0)
                codes = jnp.round(pair_of * factor).astype(jnp.int32).astype(jnp.int16)
                coded_out[chunk, half, to, :, tile * LANES : (tile + 1) * LANES] = codes
            pltpu.make_async_remote_copy(
                src_ref=scale_out.at[chunk, half],
                dst_ref=scale_in.at[chunk, half, place(half)],
                send_sem=scale_send.at[chunk, half],
                recv_sem=scale_recv.at[chunk, half],
                device_id=(along(half, step), pair),
                device_id_type=MESH,
            ).start()
            pltpu.make_async_remote_copy(
                src_ref=coded_out.at[chunk, half, to],
                dst_ref=coded_in.at[chunk, half, place(half)],
                send_sem=coded_send.at[chunk, half],
                recv_sem=coded_recv.at[chunk, half],
                device_id=(along(half, step), pair),
                device_id_type=MESH,
            ).start()

    def all_scales(chunk, half):
        return all_of(scale_in.at[chunk, half], SIDE - 1, scale_send.at[chunk, half], scale_recv.at[chunk, half])

    def all_coded(chunk, half):
        return all_of(coded_in.at[chunk, half], SIDE - 1, coded_send.at[chunk, half], coded_recv.at[chunk, half])

    def all_second(chunk, half):
        return all_of(second_in.at[chunk, half], SIDE - 1, second_send.at[chunk, half], second_recv.at[chunk, half])

    def add_first(chunk, half):
        all_scales(chunk, half).wait_recv()
        all_coded(chunk, half).wait_recv()
        own = pieces(chunk, half, place(half))
        start = tuple(jnp.concatenate([own[tile], own[tile + tiles // 2]], axis=0) for tile in range(tiles // 2))

        def add(step, totals):
            source = lax.rem(place(half) + step, SIDE)
            scale = scale_in[chunk, half, source]
            return tuple(
                total + coded_in[chunk, half, source, :, tile * LANES : (tile + 1) * LANES].astype(jnp.int32).astype(F32) * scale
                for tile, total in enumerate(totals)
            )

        totals = lax.fori_loop(1, SIDE, add, start)
        for tile, total in enumerate(totals):
            first_out[chunk, half, pl.ds(tile, SIDE, stride=tiles), :] = total[:SIDE, :]
            first_out[chunk, half, pl.ds(tile + tiles // 2, SIDE, stride=tiles), :] = total[SIDE:, :]

        @pl.loop(1, SIDE)
        def _(step):
            mine = place(1 - half)
            to = lax.rem(mine + step, SIDE)
            pltpu.make_async_remote_copy(
                src_ref=first_out.at[chunk, half, pl.ds(pl.multiple_of(to * tiles, tiles), tiles), :],
                dst_ref=second_in.at[chunk, half, mine],
                send_sem=second_send.at[chunk, half],
                recv_sem=second_recv.at[chunk, half],
                device_id=(along(1 - half, step), pair),
                device_id_type=MESH,
            ).start()

    def add_second(chunk, half):
        all_second(chunk, half).wait_recv()
        mine = place(1 - half)
        own = first_out[chunk, half, pl.ds(pl.multiple_of(mine * tiles, tiles), tiles), :]
        total = lax.fori_loop(1, SIDE, lambda step, t: t + second_in[chunk, half, lax.rem(mine + step, SIDE)], own)
        begin = (2 * chunk + half) * tiles
        panel[begin : begin + tiles, :] = total

    for turn in range(ROWS + 2):
        if turn < ROWS:
            all_pairs(turn).wait_recv()
            for half in range(2):
                multiply(turn, half)
                send_first(turn, half)
        if 0 <= turn - 1 < ROWS:
            for half in range(2):
                add_first(turn - 1, half)
        if turn == ROWS:
            for chunk in range(ROWS):
                all_pairs(chunk).wait_send()
            for chunk in range(ROWS):
                for half in range(2):
                    all_scales(chunk, half).wait_send()
                    all_coded(chunk, half).wait_send()
        if 0 <= turn - 2 < ROWS:
            for half in range(2):
                add_second(turn - 2, half)

    row = lax.broadcasted_iota(jnp.int32, (ROWS, columns), 0)
    row_gap = jnp.zeros((ROWS, columns), F32)
    for r in range(ROWS):
        row_gap = jnp.where(row == r, virt_scalar[row_vir[r]] - occ_scalar[row_occ[r]], row_gap)
    cycle = jnp.concatenate([panel[pl.ds(tile, ROWS, stride=16), :] for tile in range(columns // LANES)], axis=1)
    out_ref[...] = cycle / (row_gap + col_gap[...])
    for chunk in range(ROWS):
        for half in range(2):
            all_second(chunk, half).wait_send()


def local(
    amps,
    intermediate,
    row_irrep,
    kc_irrep,
    row_occ,
    row_vir,
    col_occ,
    col_vir,
    occ_energy,
    virt_energy,
):
    depth, columns = intermediate.shape
    vmem = pl.BlockSpec(memory_space=pltpu.VMEM)
    anywhere = pl.BlockSpec(memory_space=pltpu.HBM)
    dma = pltpu.SemaphoreType.DMA
    panel_update = pl.pallas_call(
        kernel,
        out_shape=jax.ShapeDtypeStruct((ROWS, columns), F32),
        in_specs=[anywhere] * 10,
        out_specs=vmem,
        scratch_shapes=[
            pltpu.SMEM(row_irrep.shape, jnp.int32),
            pltpu.VMEM((1, LANES), jnp.int32),
            pltpu.SMEM((ROWS,), jnp.int32),
            pltpu.SMEM((ROWS,), jnp.int32),
            pltpu.VMEM((1, columns), jnp.int32),
            pltpu.VMEM((1, columns), jnp.int32),
            pltpu.SMEM(occ_energy.shape, F32),
            pltpu.SMEM(virt_energy.shape, F32),
            pltpu.VMEM(occ_energy.shape, F32),
            pltpu.VMEM(virt_energy.shape, F32),
            pltpu.VMEM(amps.shape, BF16),
            pltpu.VMEM((depth, columns), BF16),
            pltpu.VMEM((ROWS, PAIRS, PLANE, LANES), BF16),
            pltpu.VMEM((ROWS, PLANE, depth), BF16),
            pltpu.VMEM((ROWS, PLANE, columns // 2), F32),
            pltpu.VMEM((ROWS, columns // 2 // LANES, PLANE, LANES), F32),
            pltpu.VMEM((ROWS, 2, SIDE, 16, columns // 4), jnp.int16),
            pltpu.VMEM((ROWS, 2, SIDE, 16, columns // 4), jnp.int16),
            pltpu.VMEM((ROWS, 2, 1, LANES), F32),
            pltpu.VMEM((ROWS, 2, SIDE, 1, LANES), F32),
            pltpu.VMEM((ROWS, 2, SIDE * columns // 2 // LANES, LANES), F32),
            pltpu.VMEM((ROWS, 2, SIDE, columns // 2 // LANES, LANES), F32),
            pltpu.VMEM((ROWS * columns // LANES, LANES), F32),
            pltpu.VMEM((1, 1536), F32),
            pltpu.VMEM((1, 256), F32),
            pltpu.VMEM((1, columns), F32),
            dma((10,)),
            dma,
            dma,
            dma((ROWS,)),
            dma((ROWS,)),
            dma((ROWS, 2)),
            dma((ROWS, 2)),
            dma((ROWS, 2)),
            dma((ROWS, 2)),
            dma((ROWS, 2)),
            dma((ROWS, 2)),
        ],
        compiler_params=pltpu.CompilerParams(
            collective_id=0, has_side_effects=True, vmem_limit_bytes=63 * 1024 * 1024
        ),
        cost_estimate=pl.CostEstimate(flops=2 * amps.shape[0] * amps.shape[1] * columns, bytes_accessed=9 << 20, transcendentals=0),
    )(
        amps,
        intermediate,
        row_irrep,
        kc_irrep[None, :],
        row_occ,
        row_vir,
        col_occ[None, :],
        col_vir[None, :],
        occ_energy,
        virt_energy,
    )
    return panel_update.astype(BF16)


def solution(mesh):
    return jax.shard_map(
        local,
        mesh=mesh,
        in_specs=(
            P(None, ("bulk", "pair")),
            P("bulk", None),
            P(),
            P(("bulk", "pair")),
            P(("pair", "bulk")),
            P(("pair", "bulk")),
            P(),
            P(),
            P(),
            P(),
        ),
        out_specs=P(("pair", "bulk"), None),
        check_vma=False,
    )
```

time: 94.8 us -> 65.1 us (0.69)
  the two profiles are of different devices: /device:TPU:32 before, /device:TPU:128 now
where the time goes in v2:
time: 65.1 us; the launch traced here: 64.9 us
  Pallas kernels  63.5 us (98%)
  other arithmetic  1.37 us (2%)
    pallas_call x1, Pallas kernels, local(): pl.pallas_call(kernel, out_shape=jax.ShapeDtypeStruct((ROWS, columns), F3...  63.5 us
    convert_element_type x1, other arithmetic, local(): return panel_update.astype(BF16)  1.37 us

profile of v2, /device:TPU:128, one launch (start us, length us, event | category | flops | bytes accessed | tf_op | source)
XLA Modules:
  0.0 64.9 jit_solution(14819515280257196316)
XLA Ops:
  0.0 63.5 %shard_map.100 = f32[4,2048]{1,0:T(4,128)} custom-call(bf16[4096,128]{1,0:T(8,128)(2,1)} %amps_hbm.1, bf16[2048,2048]{1,0:T(8,128)(2,1)} %weights_hbm.1, s32[4096]{0:T(1024)} %row_irrep_hbm.1, s32[1,128]{1,0:T(1,128)} %bitcast.5, s32[4]{0:T(128)} %row_occ_hbm.1, s32[4]{0:T(128)} %row_vir_hbm.1, s32[1,2048]{1,0:T(1,128)} %bitcast.3, s32[1,2048]{1,0:T(1,128)} %bitcast.4, ...), custom_call_target="tpu_custom_call" | custom-call | flops 2147483648 | bytes 9437184 | tf_op jit(solution)/shard_map/pallas_call | solution.py:357
  63.5 1.4 %convert_element_type.3 = bf16[4,2048]{1,0:T(4,128)(2,1)} convert(f32[4,2048]{1,0:T(4,128)} %shard_map.100) | non-fusion elementwise | flops 8192 | bytes 49152 | tf_op jit(solution)/shard_map/convert_element_type | solution.py:417

commit v3 on v2

--- a/solution.py
+++ b/solution.py
@@ -61,8 +61,7 @@
     weights,
     outgoing,
     regrouped,
-    sums_x,
-    sums_y,
+    sums,
     coded_out,
     coded_in,
     scale_out,
@@ -84,6 +83,8 @@
     scale_recv,
     second_send,
     second_recv,
+    pair_entered,
+    plane_entered,
 ):
     bulk = lax.axis_index("bulk")
     pair = lax.axis_index("pair")
@@ -110,36 +111,49 @@
     weights_copy = pltpu.make_async_copy(weights_hbm, weights, weights_sem)
     weights_copy.start()
 
-    def pair_peer(step):
-        return lax.rem(pair + step, PAIRS)
-
     def x_peer(step):
         return at_y * SIDE + lax.rem(at_x + step, SIDE)
 
     def y_peer(step):
         return lax.rem(at_y + step, SIDE) * SIDE + at_x
 
+    corner = lax.div(PLANE - bulk, PLANE)
+    moving = 14
+
+    def pair_at(rank):
+        return jnp.where(rank < moving, lax.rem(rank + corner, moving), rank)
+
+    pair_rank = jnp.where(pair < moving, lax.rem(pair + moving - corner, moving), pair)
+    first_pair = lax.div(PAIRS - pair, PAIRS)
+
+    def side_rank(place):
+        near = jnp.where(place <= SIDE // 2, 2 * place - 1, 2 * (SIDE - place))
+        rank = jnp.where(place == 0, 0, near)
+        return lax.rem(rank + (SIDE - 1) * first_pair, SIDE)
+
+    x_rank, y_rank = side_rank(at_x), side_rank(at_y)
+
     barrier = pltpu.get_barrier_semaphore()
 
-    @pl.loop(1, PAIRS)
-    def _(step):
-        pl.semaphore_signal(barrier, inc=1, device_id=(bulk, pair_peer(step)), device_id_type=MESH)
+    @pl.loop(pair_rank + 1, PAIRS)
+    def _(rank):
+        pl.semaphore_signal(barrier, inc=1, device_id=(bulk, pair_at(rank)), device_id_type=MESH)
 
     @pl.loop(1, SIDE)
     def _(step):
-        pl.semaphore_signal(barrier, inc=1, device_id=(x_peer(step), pair), device_id_type=MESH)
-        pl.semaphore_signal(barrier, inc=1, device_id=(y_peer(step), pair), device_id_type=MESH)
+        @pl.when(side_rank(lax.rem(at_x + step, SIDE)) > x_rank)
+        def _():
+            pl.semaphore_signal(barrier, inc=1, device_id=(x_peer(step), pair), device_id_type=MESH)
+
+        @pl.when(side_rank(lax.rem(at_y + step, SIDE)) > y_rank)
+        def _():
+            pl.semaphore_signal(barrier, inc=1, device_id=(y_peer(step), pair), device_id_type=MESH)
 
     block = ROWS * PLANE
     new_place = lax.broadcasted_iota(jnp.int32, (block, block), 0)
     old_place = lax.broadcasted_iota(jnp.int32, (block, block), 1)
     chunk_of, x_of, y_of = new_place >> 6, (new_place >> 3) & 7, new_place & 7
     reorder = jnp.where(old_place == y_of * (SIDE * ROWS) + x_of * ROWS + chunk_of, 1.0, 0.0).astype(BF16)
-    for copy in small_copies[:2]:
-        copy.wait()
-    kc = kc_irrep[...]
-
-    amps_copy.wait()
 
     def prepare(owner):
         kept = []
@@ -149,42 +163,64 @@
             begin = pl.multiple_of(owner * block + part * IRB, IRB)
             kept.append((amps[pl.ds(begin, IRB), :].astype(F32) * keep).astype(BF16))
         moved = jnp.dot(reorder, jnp.concatenate(kept, axis=0), preferred_element_type=F32).astype(BF16)
-        for chunk in range(ROWS):
-            outgoing[chunk, owner] = moved[chunk * PLANE : (chunk + 1) * PLANE, :]
-
-    @pl.loop(0, PAIRS)
-    def _(owner):
-        prepare(owner)
-
-    pl.semaphore_wait(barrier, PAIRS - 1 + 2 * (SIDE - 1))
-
-    mine_columns = pl.ds(pl.multiple_of(pair * LANES, LANES), LANES)
-
-    for chunk in range(ROWS):
-
-        @pl.loop(1, PAIRS)
-        def _(step):
-            peer = pair_peer(step)
-            pltpu.make_async_remote_copy(
-                src_ref=outgoing.at[chunk, peer],
-                dst_ref=regrouped.at[chunk, :, mine_columns],
-                send_sem=pair_send.at[chunk],
-                recv_sem=pair_recv.at[chunk],
-                device_id=(bulk, peer),
-                device_id_type=MESH,
-            ).start()
+        outgoing[owner] = moved
+
+    earlier = pair_rank + x_rank + y_rank
+
+    @pl.when(earlier > 0)
+    def _():
+        pl.semaphore_wait(barrier, earlier)
+
+    @pl.loop(0, pair_rank)
+    def _(rank):
+        pl.semaphore_signal(pair_entered.at[pair], inc=1, device_id=(bulk, pair_at(rank)), device_id_type=MESH)
+
+    @pl.loop(1, SIDE)
+    def _(step):
+        @pl.when(side_rank(lax.rem(at_x + step, SIDE)) < x_rank)
+        def _():
+            pl.semaphore_signal(plane_entered, inc=1, device_id=(x_peer(step), pair), device_id_type=MESH)
+
+        @pl.when(side_rank(lax.rem(at_y + step, SIDE)) < y_rank)
+        def _():
+            pl.semaphore_signal(plane_entered, inc=1, device_id=(y_peer(step), pair), device_id_type=MESH)
+
+    def lanes_of(source):
+        return pl.ds(pl.multiple_of(source * LANES, LANES), LANES)
+
+    def pair_copy(peer, arrival=False):
+        return pltpu.make_async_remote_copy(
+            src_ref=outgoing.at[peer],
+            dst_ref=regrouped.at[:, lanes_of(peer if arrival else pair)],
+            send_sem=pair_send,
+            recv_sem=pair_recv.at[peer if arrival else pair],
+            device_id=(bulk, peer),
+            device_id_type=MESH,
+        )
+
+    amps_copy.wait()
+    for copy in small_copies[:2]:
+        copy.wait()
+    kc = kc_irrep[...]
+
+    @pl.loop(0, PAIRS // 4)
+    def _(four):
+        peers = [pair_at(four * 4 + i) for i in range(4)]
+        for peer in peers:
+            prepare(peer)
+        for i, peer in enumerate(peers):
+
+            @pl.when(four * 4 + i < pair_rank)
+            def _():
+                pair_copy(peer).start()
+
+    regrouped[:, lanes_of(pair)] = outgoing[pair]
 
     def all_of(ref, count, send_sem, recv_sem):
         part = ref.at[pl.ds(0, count)]
         return pltpu.make_async_remote_copy(
-            src_ref=part, dst_ref=part, send_sem=send_sem, recv_sem=recv_sem, device_id=(bulk, pair_peer(1)), device_id_type=MESH
+            src_ref=part, dst_ref=part, send_sem=send_sem, recv_sem=recv_sem, device_id=(bulk, lax.rem(pair + 1, PAIRS)), device_id_type=MESH
         )
-
-    def all_pairs(chunk):
-        return all_of(outgoing.at[chunk], PAIRS - 1, pair_send.at[chunk], pair_recv.at[chunk])
-
-    for chunk in range(ROWS):
-        regrouped[chunk, :, mine_columns] = outgoing[chunk, pair]
 
     for copy in small_copies[2:]:
         copy.wait()
@@ -201,6 +237,45 @@
 
     weights_copy.wait()
 
+    def accumulate(turn, add):
+        sources = [pair_at(2 * turn), pair_at(2 * turn + 1)]
+        for source in sources:
+
+            @pl.when(source != pair)
+            def _():
+                pair_copy(source, arrival=True).wait_recv()
+
+        rows = jnp.concatenate([regrouped[:, lanes_of(source)] for source in sources], axis=1)
+
+        for tile in range(columns // width):
+            where = slice(tile * width, (tile + 1) * width)
+            factor = jnp.concatenate([weights[lanes_of(source), where] for source in sources], axis=0)
+            product = jnp.dot(rows, factor, preferred_element_type=F32)
+            for part in range(width // LANES):
+                place = tile * (width // LANES) + part
+                new = product[:, part * LANES : (part + 1) * LANES]
+                sums[place] = sums[place] + new if add else new
+
+    turns = PAIRS // 2
+
+    def greet(turn):
+        for core in range(2):
+            rank = 2 * turn + core
+            peer = pair_at(rank)
+
+            @pl.when(rank > pair_rank)
+            def _():
+                pl.semaphore_wait(pair_entered.at[peer], 1)
+                pair_copy(peer).start()
+
+    for turn in range(turns):
+        greet(turn)
+    accumulate(0, False)
+
+    @pl.loop(1, turns)
+    def _(turn):
+        accumulate(turn, True)
+
     half_width = columns // 2
     tiles = half_width // LANES
 
@@ -210,25 +285,15 @@
     def place(half):
         return at_x if half == 0 else at_y
 
-    def multiply(chunk, half):
-        @pl.loop(0, half_width // width)
-        def _(tile):
-            where = pl.ds(pl.multiple_of(half * half_width + tile * width, width), width)
-            product = jnp.dot(regrouped[chunk], weights[:, where], preferred_element_type=F32)
-            if half == 0:
-                sums_x[chunk, :, pl.ds(pl.multiple_of(tile * width, width), width)] = product
-            else:
-                for part in range(width // LANES):
-                    sums_y[chunk, tile * (width // LANES) + part] = product[:, part * LANES : (part + 1) * LANES]
-
     def pieces(chunk, half, to):
         if half == 0:
-            rows = pl.ds(pl.multiple_of(to * SIDE, SIDE), SIDE)
-            return [sums_x[chunk, rows, tile * LANES : (tile + 1) * LANES] for tile in range(tiles)]
-        return [sums_y[chunk, tile, pl.ds(to, SIDE, stride=SIDE), :] for tile in range(tiles)]
+            rows = pl.ds(pl.multiple_of(chunk * PLANE + to * SIDE, SIDE), SIDE)
+        else:
+            rows = pl.ds(chunk * PLANE + to, SIDE, stride=SIDE)
+        return [sums[half * tiles + tile, rows, :] for tile in range(tiles)]
 
     def send_first(chunk, half):
-        whole = sums_x[chunk] if half == 0 else sums_y[chunk].reshape(tiles * PLANE, LANES)
+        whole = sums[half * tiles : (half + 1) * tiles, chunk * PLANE : (chunk + 1) * PLANE, :].reshape(tiles * PLANE, LANES)
         top = jnp.maximum(jnp.max(jnp.abs(whole), axis=(0, 1), keepdims=True), 1e-33)
         scale_out[chunk, half] = jnp.broadcast_to(top * (1.0 / CODES), (1, LANES))
         factor = jnp.broadcast_to(CODES / top, (2 * SIDE, LANES))
@@ -307,25 +372,25 @@
         begin = (2 * chunk + half) * tiles
         panel[begin : begin + tiles, :] = total
 
-    for turn in range(ROWS + 2):
-        if turn < ROWS:
-            all_pairs(turn).wait_recv()
-            for half in range(2):
-                multiply(turn, half)
-                send_first(turn, half)
-        if 0 <= turn - 1 < ROWS:
-            for half in range(2):
-                add_first(turn - 1, half)
-        if turn == ROWS:
-            for chunk in range(ROWS):
-                all_pairs(chunk).wait_send()
-            for chunk in range(ROWS):
-                for half in range(2):
-                    all_scales(chunk, half).wait_send()
-                    all_coded(chunk, half).wait_send()
-        if 0 <= turn - 2 < ROWS:
-            for half in range(2):
-                add_second(turn - 2, half)
+    later_in_plane = 2 * (SIDE - 1) - x_rank - y_rank
+
+    @pl.when(later_in_plane > 0)
+    def _():
+        pl.semaphore_wait(plane_entered, later_in_plane)
+
+    for chunk in range(ROWS):
+        for half in range(2):
+            send_first(chunk, half)
+    for chunk in range(ROWS):
+        for half in range(2):
+            add_first(chunk, half)
+    for chunk in range(ROWS):
+        for half in range(2):
+            all_scales(chunk, half).wait_send()
+            all_coded(chunk, half).wait_send()
+    for chunk in range(ROWS):
+        for half in range(2):
+            add_second(chunk, half)
 
     row = lax.broadcasted_iota(jnp.int32, (ROWS, columns), 0)
     row_gap = jnp.zeros((ROWS, columns), F32)
@@ -333,6 +398,7 @@
         row_gap = jnp.where(row == r, virt_scalar[row_vir[r]] - occ_scalar[row_occ[r]], row_gap)
     cycle = jnp.concatenate([panel[pl.ds(tile, ROWS, stride=16), :] for tile in range(columns // LANES)], axis=1)
     out_ref[...] = cycle / (row_gap + col_gap[...])
+    all_of(outgoing, PAIRS - 1, pair_send, pair_recv.at[0]).wait_send()
     for chunk in range(ROWS):
         for half in range(2):
             all_second(chunk, half).wait_send()
@@ -372,10 +438,9 @@
             pltpu.VMEM(virt_energy.shape, F32),
             pltpu.VMEM(amps.shape, BF16),
             pltpu.VMEM((depth, columns), BF16),
-            pltpu.VMEM((ROWS, PAIRS, PLANE, LANES), BF16),
-            pltpu.VMEM((ROWS, PLANE, depth), BF16),
-            pltpu.VMEM((ROWS, PLANE, columns // 2), F32),
-            pltpu.VMEM((ROWS, columns // 2 // LANES, PLANE, LANES), F32),
+            pltpu.VMEM((PAIRS, ROWS * PLANE, LANES), BF16),
+            pltpu.VMEM((ROWS * PLANE, depth), BF16),
+            pltpu.VMEM((columns // LANES, ROWS * PLANE, LANES), F32),
             pltpu.VMEM((ROWS, 2, SIDE, 16, columns // 4), jnp.int16),
             pltpu.VMEM((ROWS, 2, SIDE, 16, columns // 4), jnp.int16),
             pltpu.VMEM((ROWS, 2, 1, LANES), F32),
@@ -389,14 +454,16 @@
             dma((10,)),
             dma,
             dma,
-            dma((ROWS,)),
-            dma((ROWS,)),
+            dma,
+            dma((PAIRS,)),
             dma((ROWS, 2)),
             dma((ROWS, 2)),
             dma((ROWS, 2)),
             dma((ROWS, 2)),
             dma((ROWS, 2)),
             dma((ROWS, 2)),
+            pltpu.SemaphoreType.REGULAR((PAIRS,)),
+            pltpu.SemaphoreType.REGULAR,
         ],
         compiler_params=pltpu.CompilerParams(
             collective_id=0, has_side_effects=True, vmem_limit_bytes=63 * 1024 * 1024

time: 65.1 us -> 63.5 us (0.975)
  the two profiles are of different devices: /device:TPU:128 before, /device:TPU:289 now
where the time goes in v3:
time: 63.5 us; the launch traced here: 63.3 us
  Pallas kernels  61.9 us (97%)
  other arithmetic  1.37 us (2%)
    pallas_call x1, Pallas kernels, local(): pl.pallas_call(kernel, out_shape=jax.ShapeDtypeStruct((ROWS, columns), F3...  61.9 us
    convert_element_type x1, other arithmetic, local(): return panel_update.astype(BF16)  1.37 us

profile of v3, /device:TPU:289, one launch (start us, length us, event | category | flops | bytes accessed | tf_op | source)
XLA Modules:
  0.0 63.3 jit_solution(3259311317645406446)
XLA Ops:
  0.0 61.9 %shard_map.100 = f32[4,2048]{1,0:T(4,128)} custom-call(bf16[4096,128]{1,0:T(8,128)(2,1)} %amps_hbm.1, bf16[2048,2048]{1,0:T(8,128)(2,1)} %weights_hbm.1, s32[4096]{0:T(1024)} %row_irrep_hbm.1, s32[1,128]{1,0:T(1,128)} %bitcast.5, s32[4]{0:T(128)} %row_occ_hbm.1, s32[4]{0:T(128)} %row_vir_hbm.1, s32[1,2048]{1,0:T(1,128)} %bitcast.3, s32[1,2048]{1,0:T(1,128)} %bitcast.4, ...), custom_call_target="tpu_custom_call" | custom-call | flops 2147483648 | bytes 9437184 | tf_op jit(solution)/shard_map/pallas_call | solution.py:423
  61.9 1.4 %convert_element_type.3 = bf16[4,2048]{1,0:T(4,128)(2,1)} convert(f32[4,2048]{1,0:T(4,128)} %shard_map.100) | non-fusion elementwise | flops 8192 | bytes 49152 | tf_op jit(solution)/shard_map/convert_element_type | solution.py:484

commit v4 on v3

--- a/solution.py
+++ b/solution.py
@@ -63,9 +63,12 @@
     regrouped,
     sums,
     coded_out,
-    coded_in,
+    far_in,
+    near_in,
     scale_out,
     scale_in,
+    relay_scale_out,
+    relay_scale_in,
     first_out,
     second_in,
     panel,
@@ -78,9 +81,12 @@
     pair_send,
     pair_recv,
     coded_send,
-    coded_recv,
+    far_recv,
+    near_recv,
     scale_send,
     scale_recv,
+    relay_scale_send,
+    relay_scale_recv,
     second_send,
     second_recv,
     pair_entered,
@@ -292,61 +298,116 @@
             rows = pl.ds(chunk * PLANE + to, SIDE, stride=SIDE)
         return [sums[half * tiles + tile, rows, :] for tile in range(tiles)]
 
-    def send_first(chunk, half):
-        whole = sums[half * tiles : (half + 1) * tiles, chunk * PLANE : (chunk + 1) * PLANE, :].reshape(tiles * PLANE, LANES)
+    ahead = (1, SIDE - 1, 2, SIDE - 2)
+    quarter = tiles // 2
+
+    def joined(given):
+        return [jnp.concatenate([given[tile], given[tile + quarter]], axis=0) for tile in range(quarter)]
+
+    def block_for(chunk, half, step):
+        return joined(pieces(chunk, half, lax.rem(place(half) + step, SIDE)))
+
+    def store_codes(chunk, half, slot, blocks, factor):
+        for tile, value in enumerate(blocks):
+            codes = jnp.round(value * factor).astype(jnp.int32).astype(jnp.int16)
+            coded_out[chunk, half, slot, :, tile * LANES : (tile + 1) * LANES] = codes
+
+    def first_copy(chunk, half, slot, target, recv_sem, step, lanes=slice(None)):
+        return pltpu.make_async_remote_copy(
+            src_ref=coded_out.at[chunk, half, slot, :, lanes],
+            dst_ref=target.at[:, lanes],
+            send_sem=coded_send.at[chunk, half],
+            recv_sem=recv_sem.at[chunk, half],
+            device_id=(along(half, step), pair),
+            device_id_type=MESH,
+        )
+
+    later_in_plane = 2 * (SIDE - 1) - x_rank - y_rank
+
+    @pl.when(later_in_plane > 0)
+    def _():
+        pl.semaphore_wait(plane_entered, later_in_plane)
+
+    factors = []
+    for half in range(2):
+        whole = sums[half * tiles : (half + 1) * tiles].reshape(tiles * block, LANES)
         top = jnp.maximum(jnp.max(jnp.abs(whole), axis=(0, 1), keepdims=True), 1e-33)
-        scale_out[chunk, half] = jnp.broadcast_to(top * (1.0 / CODES), (1, LANES))
-        factor = jnp.broadcast_to(CODES / top, (2 * SIDE, LANES))
-
-        @pl.loop(1, SIDE)
-        def _(step):
-            to = lax.rem(place(half) + step, SIDE)
-            given = pieces(chunk, half, to)
-            for tile in range(tiles // 2):
-                pair_of = jnp.concatenate([given[tile], given[tile + tiles // 2]], axis=0)
-                codes = jnp.round(pair_of * factor).astype(jnp.int32).astype(jnp.int16)
-                coded_out[chunk, half, to, :, tile * LANES : (tile + 1) * LANES] = codes
+        scale_out[half] = jnp.broadcast_to(top * (1.0 / CODES), (1, LANES))
+        factors.append(jnp.broadcast_to(CODES / top, (2 * SIDE, LANES)))
+        for slot, step in enumerate(ahead):
             pltpu.make_async_remote_copy(
-                src_ref=scale_out.at[chunk, half],
-                dst_ref=scale_in.at[chunk, half, place(half)],
-                send_sem=scale_send.at[chunk, half],
-                recv_sem=scale_recv.at[chunk, half],
+                src_ref=scale_out.at[half],
+                dst_ref=scale_in.at[half, slot],
+                send_sem=scale_send.at[half],
+                recv_sem=scale_recv.at[half],
                 device_id=(along(half, step), pair),
                 device_id_type=MESH,
             ).start()
+
+    left, right = slice(0, quarter * LANES // 2), slice(quarter * LANES // 2, quarter * LANES)
+
+    @pl.loop(0, ROWS)
+    def _(chunk):
+        for half in range(2):
+            for slot, step in ((0, 3), (1, SIDE - 3), (2, 4)):
+                store_codes(chunk, half, slot, block_for(chunk, half, step), factors[half])
+            first_copy(chunk, half, 0, far_in.at[chunk, half, 0], far_recv, 1).start()
+            first_copy(chunk, half, 1, far_in.at[chunk, half, 1], far_recv, SIDE - 1).start()
+            first_copy(chunk, half, 2, far_in.at[chunk, half, 2], far_recv, 2, left).start()
+            first_copy(chunk, half, 2, far_in.at[chunk, half, 2], far_recv, SIDE - 2, right).start()
+
+    @pl.loop(0, ROWS)
+    def _(chunk):
+        for half in range(2):
+            for slot, step in ((3, 1), (4, SIDE - 1)):
+                store_codes(chunk, half, slot, block_for(chunk, half, step), factors[half])
+                first_copy(chunk, half, slot, near_in.at[chunk, half, slot - 3], near_recv, step).start()
+
+    relay_factors = []
+    for half in range(2):
+        all_of(scale_in.at[half], 4, scale_send.at[half], scale_recv.at[half]).wait_recv()
+        for way in range(2):
+            bound = scale_out[half] + scale_in[half, way] + scale_in[half, 2 + way]
+            relay_scale_out[half, way] = bound
+            relay_factors.append(jnp.broadcast_to(1.0 / bound, (2 * SIDE, LANES)))
             pltpu.make_async_remote_copy(
-                src_ref=coded_out.at[chunk, half, to],
-                dst_ref=coded_in.at[chunk, half, place(half)],
-                send_sem=coded_send.at[chunk, half],
-                recv_sem=coded_recv.at[chunk, half],
-                device_id=(along(half, step), pair),
+                src_ref=relay_scale_out.at[half, way],
+                dst_ref=relay_scale_in.at[half, way],
+                send_sem=relay_scale_send.at[half],
+                recv_sem=relay_scale_recv.at[half],
+                device_id=(along(half, ahead[2 + way]), pair),
                 device_id_type=MESH,
             ).start()
 
-    def all_scales(chunk, half):
-        return all_of(scale_in.at[chunk, half], SIDE - 1, scale_send.at[chunk, half], scale_recv.at[chunk, half])
-
-    def all_coded(chunk, half):
-        return all_of(coded_in.at[chunk, half], SIDE - 1, coded_send.at[chunk, half], coded_recv.at[chunk, half])
+    def values(ref, chunk, half, slot, tile):
+        return ref[chunk, half, slot, :, tile * LANES : (tile + 1) * LANES].astype(jnp.int32).astype(F32)
+
+    @pl.loop(0, ROWS)
+    def _(chunk):
+        for half in range(2):
+            all_of(far_in.at[chunk, half], 3, coded_send.at[chunk, half], far_recv.at[chunk, half]).wait_recv()
+            for way in range(2):
+                totals = block_for(chunk, half, ahead[2 + way])
+                for tile in range(quarter):
+                    totals[tile] = totals[tile] + values(far_in, chunk, half, way, tile) * scale_in[half, way]
+                    if tile // (quarter // 2) == way:
+                        totals[tile] = totals[tile] + values(far_in, chunk, half, 2, tile) * scale_in[half, 2 + way]
+                store_codes(chunk, half, 5 + way, totals, relay_factors[2 * half + way])
+                first_copy(chunk, half, 5 + way, near_in.at[chunk, half, 2 + way], near_recv, ahead[2 + way]).start()
+
+    for half in range(2):
+        all_of(relay_scale_in.at[half], 2, relay_scale_send.at[half], relay_scale_recv.at[half]).wait_recv()
 
     def all_second(chunk, half):
         return all_of(second_in.at[chunk, half], SIDE - 1, second_send.at[chunk, half], second_recv.at[chunk, half])
 
     def add_first(chunk, half):
-        all_scales(chunk, half).wait_recv()
-        all_coded(chunk, half).wait_recv()
-        own = pieces(chunk, half, place(half))
-        start = tuple(jnp.concatenate([own[tile], own[tile + tiles // 2]], axis=0) for tile in range(tiles // 2))
-
-        def add(step, totals):
-            source = lax.rem(place(half) + step, SIDE)
-            scale = scale_in[chunk, half, source]
-            return tuple(
-                total + coded_in[chunk, half, source, :, tile * LANES : (tile + 1) * LANES].astype(jnp.int32).astype(F32) * scale
-                for tile, total in enumerate(totals)
-            )
-
-        totals = lax.fori_loop(1, SIDE, add, start)
+        all_of(near_in.at[chunk, half], 4, coded_send.at[chunk, half], near_recv.at[chunk, half]).wait_recv()
+        totals = block_for(chunk, half, 0)
+        for tile in range(quarter):
+            for slot in range(4):
+                scale = scale_in[half, slot] if slot < 2 else relay_scale_in[half, slot - 2]
+                totals[tile] = totals[tile] + values(near_in, chunk, half, slot, tile) * scale
         for tile, total in enumerate(totals):
             first_out[chunk, half, pl.ds(tile, SIDE, stride=tiles), :] = total[:SIDE, :]
             first_out[chunk, half, pl.ds(tile + tiles // 2, SIDE, stride=tiles), :] = total[SIDE:, :]
@@ -369,26 +430,15 @@
         mine = place(1 - half)
         own = first_out[chunk, half, pl.ds(pl.multiple_of(mine * tiles, tiles), tiles), :]
         total = lax.fori_loop(1, SIDE, lambda step, t: t + second_in[chunk, half, lax.rem(mine + step, SIDE)], own)
-        begin = (2 * chunk + half) * tiles
-        panel[begin : begin + tiles, :] = total
-
-    later_in_plane = 2 * (SIDE - 1) - x_rank - y_rank
-
-    @pl.when(later_in_plane > 0)
-    def _():
-        pl.semaphore_wait(plane_entered, later_in_plane)
-
-    for chunk in range(ROWS):
-        for half in range(2):
-            send_first(chunk, half)
-    for chunk in range(ROWS):
+        panel[pl.ds(pl.multiple_of((2 * chunk + half) * tiles, tiles), tiles), :] = total
+
+    @pl.loop(0, ROWS)
+    def _(chunk):
         for half in range(2):
             add_first(chunk, half)
-    for chunk in range(ROWS):
-        for half in range(2):
-            all_scales(chunk, half).wait_send()
-            all_coded(chunk, half).wait_send()
-    for chunk in range(ROWS):
+
+    @pl.loop(0, ROWS)
+    def _(chunk):
         for half in range(2):
             add_second(chunk, half)
 
@@ -399,8 +449,14 @@
     cycle = jnp.concatenate([panel[pl.ds(tile, ROWS, stride=16), :] for tile in range(columns // LANES)], axis=1)
     out_ref[...] = cycle / (row_gap + col_gap[...])
     all_of(outgoing, PAIRS - 1, pair_send, pair_recv.at[0]).wait_send()
-    for chunk in range(ROWS):
+    for half in range(2):
+        all_of(scale_in.at[half], 4, scale_send.at[half], scale_recv.at[half]).wait_send()
+        all_of(relay_scale_in.at[half], 2, relay_scale_send.at[half], relay_scale_recv.at[half]).wait_send()
+
+    @pl.loop(0, ROWS)
+    def _(chunk):
         for half in range(2):
+            all_of(coded_out.at[chunk, half], 7, coded_send.at[chunk, half], far_recv.at[chunk, half]).wait_send()
             all_second(chunk, half).wait_send()
 
 
@@ -441,10 +497,13 @@
             pltpu.VMEM((PAIRS, ROWS * PLANE, LANES), BF16),
             pltpu.VMEM((ROWS * PLANE, depth), BF16),
             pltpu.VMEM((columns // LANES, ROWS * PLANE, LANES), F32),
-            pltpu.VMEM((ROWS, 2, SIDE, 16, columns // 4), jnp.int16),
-            pltpu.VMEM((ROWS, 2, SIDE, 16, columns // 4), jnp.int16),
-            pltpu.VMEM((ROWS, 2, 1, LANES), F32),
-            pltpu.VMEM((ROWS, 2, SIDE, 1, LANES), F32),
+            pltpu.VMEM((ROWS, 2, 7, 16, columns // 4), jnp.int16),
+            pltpu.VMEM((ROWS, 2, 3, 16, columns // 4), jnp.int16),
+            pltpu.VMEM((ROWS, 2, 4, 16, columns // 4), jnp.int16),
+            pltpu.VMEM((2, 1, LANES), F32),
+            pltpu.VMEM((2, 4, 1, LANES), F32),
+            pltpu.VMEM((2, 2, 1, LANES), F32),
+            pltpu.VMEM((2, 2, 1, LANES), F32),
             pltpu.VMEM((ROWS, 2, SIDE * columns // 2 // LANES, LANES), F32),
             pltpu.VMEM((ROWS, 2, SIDE, columns // 2 // LANES, LANES), F32),
             pltpu.VMEM((ROWS * columns // LANES, LANES), F32),
@@ -459,7 +518,10 @@
             dma((ROWS, 2)),
             dma((ROWS, 2)),
             dma((ROWS, 2)),
-            dma((ROWS, 2)),
+            dma((2,)),
+            dma((2,)),
+            dma((2,)),
+            dma((2,)),
             dma((ROWS, 2)),
             dma((ROWS, 2)),
             pltpu.SemaphoreType.REGULAR((PAIRS,)),

time: 63.5 us -> 58.4 us (0.920)
  the two profiles are of different devices: /device:TPU:289 before, /device:TPU:273 now
where the time goes in v4:
time: 58.4 us; the launch traced here: 58.2 us
  Pallas kernels  56.8 us (97%)
  other arithmetic  1.37 us (2%)
    pallas_call x1, Pallas kernels, local(): pl.pallas_call(kernel, out_shape=jax.ShapeDtypeStruct((ROWS, columns), F3...  56.8 us
    convert_element_type x1, other arithmetic, local(): return panel_update.astype(BF16)  1.37 us

profile of v4, /device:TPU:273, one launch (start us, length us, event | category | flops | bytes accessed | tf_op | source)
XLA Modules:
  0.0 58.2 jit_solution(11611268347603802838)
XLA Ops:
  0.0 56.8 %shard_map.100 = f32[4,2048]{1,0:T(4,128)} custom-call(bf16[4096,128]{1,0:T(8,128)(2,1)} %amps_hbm.1, bf16[2048,2048]{1,0:T(8,128)(2,1)} %weights_hbm.1, s32[4096]{0:T(1024)} %row_irrep_hbm.1, s32[1,128]{1,0:T(1,128)} %bitcast.5, s32[4]{0:T(128)} %row_occ_hbm.1, s32[4]{0:T(128)} %row_vir_hbm.1, s32[1,2048]{1,0:T(1,128)} %bitcast.3, s32[1,2048]{1,0:T(1,128)} %bitcast.4, ...), custom_call_target="tpu_custom_call" | custom-call | flops 2147483648 | bytes 9437184 | tf_op jit(solution)/shard_map/pallas_call | solution.py:479
  56.8 1.4 %convert_element_type.3 = bf16[4,2048]{1,0:T(4,128)(2,1)} convert(f32[4,2048]{1,0:T(4,128)} %shard_map.100) | non-fusion elementwise | flops 8192 | bytes 49152 | tf_op jit(solution)/shard_map/convert_element_type | solution.py:546

commit v5 on v4

--- a/solution.py
+++ b/solution.py
@@ -115,7 +115,6 @@
     for copy in small_copies:
         copy.start()
     weights_copy = pltpu.make_async_copy(weights_hbm, weights, weights_sem)
-    weights_copy.start()
 
     def x_peer(step):
         return at_y * SIDE + lax.rem(at_x + step, SIDE)
@@ -205,6 +204,7 @@
         )
 
     amps_copy.wait()
+    weights_copy.start()
     for copy in small_copies[:2]:
         copy.wait()
     kc = kc_irrep[...]
@@ -437,6 +437,16 @@
         for half in range(2):
             add_first(chunk, half)
 
+    all_of(outgoing, PAIRS - 1, pair_send, pair_recv.at[0]).wait_send()
+    for half in range(2):
+        all_of(scale_in.at[half], 4, scale_send.at[half], scale_recv.at[half]).wait_send()
+        all_of(relay_scale_in.at[half], 2, relay_scale_send.at[half], relay_scale_recv.at[half]).wait_send()
+
+    @pl.loop(0, ROWS)
+    def _(chunk):
+        for half in range(2):
+            all_of(coded_out.at[chunk, half], 7, coded_send.at[chunk, half], far_recv.at[chunk, half]).wait_send()
+
     @pl.loop(0, ROWS)
     def _(chunk):
         for half in range(2):
@@ -448,15 +458,10 @@
         row_gap = jnp.where(row == r, virt_scalar[row_vir[r]] - occ_scalar[row_occ[r]], row_gap)
     cycle = jnp.concatenate([panel[pl.ds(tile, ROWS, stride=16), :] for tile in range(columns // LANES)], axis=1)
     out_ref[...] = cycle / (row_gap + col_gap[...])
-    all_of(outgoing, PAIRS - 1, pair_send, pair_recv.at[0]).wait_send()
-    for half in range(2):
-        all_of(scale_in.at[half], 4, scale_send.at[half], scale_recv.at[half]).wait_send()
-        all_of(relay_scale_in.at[half], 2, relay_scale_send.at[half], relay_scale_recv.at[half]).wait_send()
-
-    @pl.loop(0, ROWS)
-    def _(chunk):
-        for half in range(2):
-            all_of(coded_out.at[chunk, half], 7, coded_send.at[chunk, half], far_recv.at[chunk, half]).wait_send()
+
+    @pl.loop(0, ROWS)
+    def _(chunk):
+        for half in range(2):
             all_second(chunk, half).wait_send()
 
 

time: 58.4 us -> 58.3 us (level)
  no operation moved by 1% of the time
where the time goes in v5:
time: 58.3 us; the launch traced here: 58.1 us
  Pallas kernels  56.7 us (97%)
  other arithmetic  1.37 us (2%)
    pallas_call x1, Pallas kernels, local(): pl.pallas_call(kernel, out_shape=jax.ShapeDtypeStruct((ROWS, columns), F3...  56.7 us
    convert_element_type x1, other arithmetic, local(): return panel_update.astype(BF16)  1.37 us

profile of v5, /device:TPU:273, one launch (start us, length us, event | category | flops | bytes accessed | tf_op | source)
XLA Modules:
  0.0 58.1 jit_solution(4133570235228680873)
XLA Ops:
  0.0 56.7 %shard_map.100 = f32[4,2048]{1,0:T(4,128)} custom-call(bf16[4096,128]{1,0:T(8,128)(2,1)} %amps_hbm.1, bf16[2048,2048]{1,0:T(8,128)(2,1)} %weights_hbm.1, s32[4096]{0:T(1024)} %row_irrep_hbm.1, s32[1,128]{1,0:T(1,128)} %bitcast.5, s32[4]{0:T(128)} %row_occ_hbm.1, s32[4]{0:T(128)} %row_vir_hbm.1, s32[1,2048]{1,0:T(1,128)} %bitcast.3, s32[1,2048]{1,0:T(1,128)} %bitcast.4, ...), custom_call_target="tpu_custom_call" | custom-call | flops 2147483648 | bytes 9437184 | tf_op jit(solution)/shard_map/pallas_call | solution.py:484
  56.7 1.4 %convert_element_type.3 = bf16[4,2048]{1,0:T(4,128)(2,1)} convert(f32[4,2048]{1,0:T(4,128)} %shard_map.100) | non-fusion elementwise | flops 8192 | bytes 49152 | tf_op jit(solution)/shard_map/convert_element_type | solution.py:551
